TPU v7x, 32 devices: a whole 2x2x4 slice. The times are simulated.
32 devices in a mesh: tok: 4 (over y, core), voc: 8 (over z, x).
Axes of the slice: x: 2, y: 2, z: 4, core: 2. Of those that a mesh axis runs over, the one named last changes fastest.
Arguments:
- hidden: bfloat16 [512, 2880], P('tok'), may hold values from -40 to 40
- frozen_head_weight: bfloat16 [2880, 201088], P(None, ('tok', 'voc')), may hold values from -2 to 2
- adapter_down: bfloat16 [2880, 32], replicated, may hold values from -1 to 1
- adapter_up: bfloat16 [32, 201088], P(None, ('tok', 'voc')), may hold values from -1.5 to 1.5
- targets: int32 [512], P('tok'), may hold values from 0 to 201087
- segment: int32 [512], P('tok'), may hold values from 0 to 15, as said below
- response: int32 [512], P('tok'), may hold values from 0 to 1, as said below
- chosen_first: int32 [8], replicated, may hold values 0 or 1
- reference_logp: float32 [16], replicated, may hold values from -20 to -17
Outputs:
- log_ratio: float32 [16], replicated
- hidden_gradient: bfloat16 [512, 2880], P('tok', 'voc')
- adapter_down_gradient: float32 [2880, 32], replicated
- adapter_up_gradient: float32 [32, 201088], P(None, ('tok', 'voc'))
Inputs may be any that keep to these rules, and one draw needn't show every extreme that they name: `segment`: sequence numbers never fall; every sequence has an even length of 2 or more; the rows of one index of tok hold exactly 4 whole sequences; sequences 2p and 2p+1 form pair p. The response rows of a sequence are its last rows, 1 to half of its length of them; the rows of one index of tok hold at most 64 response rows, and some index holds exactly 64.
All inputs are finite; a program needn't handle non-finite values.
Results may differ from a plain program's by a relative error of at most 0.0072.
Values may be sent and summed in bfloat16 or wider, within the bound.
A program may use at most 128 MiB of HBM per device.

v0:
```python
import jax
import jax.numpy as jnp
from jax import lax
from jax.sharding import PartitionSpec as P

adapter_scale = 2.0
target_margin = 10.0


def merged(value, axis, join):
    pieces = jax.tree.map(lambda part: lax.all_gather(part, axis), value)
    head = jax.tree.map(lambda part: part[0], pieces)
    tail = jax.tree.map(lambda part: part[1:], pieces)
    subtotal, _ = lax.scan(lambda subtotal, slab: (join(subtotal, slab), None), head, tail)
    return subtotal


def contract_dims(left, right, left_dim, right_dim):
    return lax.dot_general(
        left, right, (((left_dim,), (right_dim,)), ((), ())), preferred_element_type=jnp.float32
    )


def combine_stats(earlier, later):
    peak = jnp.maximum(earlier[0], later[0])
    summed = earlier[1] * jnp.exp(earlier[0] - peak) + later[1] * jnp.exp(later[0] - peak)
    return (peak, summed, earlier[2] + later[2])


def on_device(
    hidden,
    frozen_head_weight,
    adapter_down,
    adapter_up,
    targets,
    segment,
    response,
    chosen_first,
    reference_logp,
):
    voc_count = lax.axis_size("voc")
    token_index = lax.axis_index("tok")
    voc_index = lax.axis_index("voc")
    vocab_width = frozen_head_weight.shape[1]
    vocab_start = (token_index * voc_count + voc_index) * vocab_width
    feature_width = hidden.shape[1] // voc_count
    slot_order = jnp.argsort(1 - response, stable=True)[: hidden.shape[0] // 2]
    local_rows = hidden[slot_order]
    labels = jnp.stack([targets[slot_order], segment[slot_order], response[slot_order]])
    row_block_slice = local_rows.shape[0]
    gathered_rows = lax.all_gather(local_rows, "tok", axis=0, tiled=True)
    all_labels = lax.all_gather(labels, "tok", axis=1, tiled=True)
    target_ids = all_labels[0]
    segment_ids = all_labels[1]
    live = all_labels[2].astype(jnp.float32)
    adapter_input = jnp.dot(gathered_rows, adapter_down, preferred_element_type=jnp.float32).astype(
        jnp.bfloat16
    )
    logit_matrix = jnp.dot(
        gathered_rows, frozen_head_weight, preferred_element_type=jnp.float32
    ) + adapter_scale * jnp.dot(adapter_input, adapter_up, preferred_element_type=jnp.float32)
    local_peak = jnp.max(logit_matrix, axis=1)
    local_summed = jnp.sum(jnp.exp(logit_matrix - local_peak[:, None]), axis=1)
    column_slot = target_ids - vocab_start
    owned = (column_slot >= 0) & (column_slot < vocab_width)
    column_slot = jnp.clip(column_slot, 0, vocab_width - 1)
    picked = jnp.take_along_axis(logit_matrix, column_slot[:, None], axis=1)[:, 0]
    picked = jnp.where(owned, picked, 0.0)
    peak, summed, target_logit = merged(
        (local_peak, local_summed, picked), ("tok", "voc"), combine_stats
    )
    log_partition = peak + jnp.log(summed)
    token_log_probability = target_logit - log_partition
    seq_count = reference_logp.shape[0]
    member = (segment_ids[:, None] == jnp.arange(seq_count, dtype=jnp.int32)[None, :]).astype(
        jnp.float32
    )
    counts = jnp.sum(member * live[:, None], axis=0)
    totals = jnp.sum(member * (token_log_probability * live)[:, None], axis=0)
    log_ratio = totals / counts - reference_logp
    pairs = log_ratio.reshape(-1, 2)
    first_wins = chosen_first == 1
    margin = jnp.where(first_wins, pairs[:, 0] - pairs[:, 1], pairs[:, 1] - pairs[:, 0])
    slope = 2.0 * (margin - target_margin)
    ratio_grad = jnp.stack(
        [jnp.where(first_wins, slope, -slope), jnp.where(first_wins, -slope, slope)], axis=1
    ).reshape(-1)
    row_weight = live * jnp.sum(member * (ratio_grad / counts)[None, :], axis=1)
    predicted = jnp.exp(logit_matrix - log_partition[:, None])
    hits = (jnp.arange(vocab_width, dtype=jnp.int32)[None, :] == column_slot[:, None]) & owned[
        :, None
    ]
    logit_gradient = (row_weight[:, None] * (predicted - hits.astype(jnp.float32))).astype(
        jnp.bfloat16
    )
    adapter_up_gradient = adapter_scale * contract_dims(adapter_input, logit_gradient, 0, 0)
    adapter_gradient = lax.psum(
        adapter_scale * contract_dims(logit_gradient, adapter_up, 1, 1), ("tok", "voc")
    ).astype(jnp.bfloat16)
    adapter_down_gradient = contract_dims(gathered_rows, adapter_gradient, 0, 0)
    partial_grad = contract_dims(logit_gradient, frozen_head_weight, 1, 1)
    reduced_sum = lax.psum_scatter(partial_grad, "voc", scatter_dimension=1, tiled=True)
    reduced_sum = lax.psum_scatter(reduced_sum, "tok", scatter_dimension=0, tiled=True)
    local_adapter_rows = lax.dynamic_slice_in_dim(
        adapter_gradient, token_index * row_block_slice, row_block_slice, 0
    )
    local_adapter = lax.dynamic_slice_in_dim(
        adapter_down, voc_index * feature_width, feature_width, 0
    )
    slot_gradient = reduced_sum + contract_dims(local_adapter_rows, local_adapter, 1, 1)
    row_grad = (
        jnp.zeros((hidden.shape[0], feature_width), jnp.float32).at[slot_order].set(slot_gradient)
    )
    hidden_gradient = row_grad.astype(jnp.bfloat16)
    return (log_ratio, hidden_gradient, adapter_down_gradient, adapter_up_gradient)


def solution(mesh):
    in_specs = (
        P("tok", None),
        P(None, ("tok", "voc")),
        P(),
        P(None, ("tok", "voc")),
        P("tok"),
        P("tok"),
        P("tok"),
        P(),
        P(),
    )
    out_specs = (P(), P("tok", "voc"), P(), P(None, ("tok", "voc")))
    return jax.shard_map(
        on_device, mesh=mesh, in_specs=in_specs, out_specs=out_specs, check_vma=False
    )
```

profile of v0, /device:TPU:16, one launch (start us, length us, event | category | flops | bytes accessed | tf_op | source)
XLA Modules:
  0.0 426.2 jit_solution(15179894913811640511)
XLA Ops:
  7.2 0.0 copy-start
  7.2 0.0 copy-start.1
  7.2 0.0 copy-start.4
  7.2 0.0 all-gather.9.cloned.1.call-start
  7.2 0.7 broadcast_subtract_fusion
  8.0 2.5 sort.17
  10.5 1.5 copy.28
  12.0 1.5 gather_fusion.3
  13.5 0.0 all-gather.9.cloned.1.call-update
  13.5 0.0 reduce-scatter.5.cloned.1.call-start
  13.6 1.4 gather_fusion.2
  15.0 1.4 gather_fusion.1
  16.5 0.0 copy-done.1
  16.5 0.8 gather_fusion
  17.3 5.2 %all-gather.3 = s32[4,64,3]{1,2,0:T(4,128)S(1)} all-gather(s32[1,64,3]{1,2,0:T(4,128)S(1)} %add_bitcast_fusion), channel_id=1, replica_groups=mesh['tok'=4,'voc'=8] {'tok'}, dimensions={0}, use_global_device_ids=true | all-gather | bytes 3840 | tf_op jit(solution)/shard_map/all_gather | solution.py:52
  22.4 0.1 reshape.181
  22.6 11.5 %all-gather.9.cloned.1.call-done = bf16[256,2880]{1,0:T(8,128)(2,1)} async-done(((bf16[64,2880]{1,0:T(8,128)(2,1)}), bf16[256,2880]{1,0:T(8,128)(2,1)}) %all-gather.9.cloned.1.call-update) | async-done | bytes 1474576 | tf_op jit(solution)/shard_map/all_gather | solution.py:51
  34.1 0.0 copy-done.4
  34.1 1.9 convolution_convert_fusion
  36.0 21.9 %fusion.17 = f32[256,6284]{0,1:T(8,128)} fusion(bf16[256,2880]{1,0:T(8,128)(2,1)} %all-gather.9.cloned.1.call-done, bf16[2880,6284]{1,0:T(8,128)(2,1)} %param.12), kind=kOutput, calls=%fused_computation.66 | convolution fusion | flops 9266135040 | bytes 44105216 | tf_op jit(solution)/shard_map/dot_general | solution.py:59
  57.9 0.0 copy-done
  57.9 4.1 fusion.16
  62.0 0.0 copy-start.2
  62.0 0.0 copy-start.7
  62.0 0.0 copy-start.6
  62.0 2.7 copy-done.2
  64.7 0.9 exponential_reduce_fusion
  65.6 61.9 %all-gather.5 = f32[32,1,256]{2,1,0:T(1,128)S(1)} all-gather(f32[1,1,256]{2,1,0:T(1,128)S(1)} %bitcast.85), channel_id=4, replica_groups=mesh['tok'=4,'voc'=8] {'tok','voc'}, dimensions={0}, use_global_device_ids=true | all-gather | bytes 33792 | tf_op jit(solution)/shard_map/all_gather | solution.py:11
  127.5 8.0 %gather_fusion.4 = f32[256]{0:T(256)S(1)} fusion(f32[256,6284]{0,1:T(8,128)} %copy-done.2, s32[256]{0:T(256)S(1)} %bitcast.64), kind=kCustom, calls=%fused_computation.4 | custom fusion | bytes 4096 | tf_op jit(solution)/shard_map/jit(take_along_axis)/gather | solution.py:67
  135.5 64.8 %all-gather.6 = f32[32,1,256]{2,1,0:T(1,128)S(1)} all-gather(f32[1,1,256]{2,1,0:T(1,128)S(1)} %fusion.10), channel_id=1, replica_groups=mesh['tok'=4,'voc'=8] {'tok','voc'}, dimensions={0}, use_global_device_ids=true | all-gather | bytes 33792 | tf_op jit(solution)/shard_map/all_gather | solution.py:11
  200.3 65.8 %all-gather.4 = f32[32,1,256]{2,1,0:T(1,128)S(1)} all-gather(f32[1,1,256]{2,1,0:T(1,128)S(1)} %bitcast.84), channel_id=3, replica_groups=mesh['tok'=4,'voc'=8] {'tok','voc'}, dimensions={0}, use_global_device_ids=true | all-gather | bytes 33792 | tf_op jit(solution)/shard_map/all_gather | solution.py:11
  266.2 2.6 while.14
  268.8 0.1 select_reduce_fusion.1
  268.9 0.0 copy-done.7
  269.0 0.0 copy-start.5
  269.0 0.1 reshape.115
  269.0 0.2 subtract_reduce_fusion
  269.2 0.0 copy-done.6
  269.3 0.1 copy.29
  269.4 0.1 reshape.116
  269.4 0.1 select_reduce_fusion
  269.5 6.8 %multiply_convert_fusion = bf16[256,6284]{0,1:T(8,128)(2,1)} fusion(f32[256,6284]{0,1:T(8,128)} %copy-done.2, s32[256]{0:T(256)S(1)} %bitcast.81, f32[256]{0:T(256)S(1)} %get-tuple-element.81, f32[256]{0:T(256)S(1)} %mul.93, pred[256]{0:T(512)(128)(4,1)S(1)} %fusion.14), kind=kLoop, calls=%fused_computation.13 | loop fusion | flops 11260928 | bytes 9655552 | tf_op jit(solution)/shard_map/convert_element_type | solution.py:93
  276.3 18.3 %fusion.18 = f32[256,2880]{0,1:T(8,128)} fusion(bf16[256,6284]{0,1:T(8,128)(2,1)} %multiply_convert_fusion, bf16[2880,6284]{1,0:T(8,128)(2,1)} %param.12), kind=kOutput, calls=%fused_computation.67 | convolution fusion | flops 9266135040 | bytes 42362368 | tf_op jit(solution)/shard_map/dot_general | solution.py:19
  294.6 0.0 copy-done.5
  294.6 0.0 copy-start.3
  294.6 0.0 reduce-scatter.5.cloned.1.call-update
  294.6 0.0 reduce-scatter.7.cloned.1.call-start
  294.7 73.2 %reduce-scatter.5.cloned.1.call-done = f32[256,360]{0,1:T(8,128)} async-done(((f32[256,2880]{0,1:T(8,128)}), f32[256,360]{0,1:T(8,128)}) %reduce-scatter.5.cloned.1.call-update) | async-done | bytes 368656 | tf_op jit(solution)/shard_map/reduce_scatter | solution.py:102
  367.9 1.9 copy.32
  369.8 0.0 reduce-scatter.7.cloned.1.call-update
  369.8 2.5 convolution_multiply_fusion.2
  372.3 39.5 %psum.7 = bf16[256,32]{0,1:T(8,128)(2,1)S(1)} all-reduce(f32[256,32]{0,1:T(8,128)S(1)} %convolution_multiply_fusion.2), channel_id=1, replica_groups=mesh['tok'=4,'voc'=8] {'tok','voc'}, use_global_device_ids=true, to_apply=%region_10.11 | all-reduce | flops 8192 | bytes 49152 | tf_op jit(solution)/shard_map/psum | solution.py:97
  411.9 0.0 copy-done.3
  411.9 1.1 fusion.19
  413.0 3.9 convolution_multiply_fusion.1
  416.9 0.0 reduce-scatter.7.cloned.1.call-done
  416.9 1.1 convolution_add_fusion
  418.0 0.9 scatter_custom_fusion
  418.9 0.7 copy.31
  (152 shorter events, 1.9 us)
Async XLA Ops:
  7.2 50.7 %copy-start = (bf16[32,6284]{1,0:T(8,128)(2,1)S(1)}, bf16[32,6284]{1,0:T(8,128)(2,1)}, u32[]{:S(2)}) copy-start(bf16[32,6284]{1,0:T(8,128)(2,1)} %param.14) | copy-start | bytes 1206532
  7.2 9.3 %copy-start.1 = (s32[128]{0:T(128)S(1)}, s32[128]{0:T(128)}, u32[]{:S(2)}) copy-start(s32[128]{0:T(128)} %param.15) | copy-start | bytes 1540
  7.2 26.9 %copy-start.4 = (bf16[2880,32]{0,1:T(8,128)(2,1)S(1)}, bf16[2880,32]{0,1:T(8,128)(2,1)}, u32[]{:S(2)}) copy-start(bf16[2880,32]{0,1:T(8,128)(2,1)} %param.13) | copy-start | bytes 552964
  7.2 26.9 %all-gather.9.cloned.1.call-start = ((), (), s32[]{:S(2)}) async-start(), calls=%async_computation.3 | async-start | bytes 1884160 | tf_op jit(solution)/shard_map/all_gather | solution.py:51
  13.5 354.4 %reduce-scatter.5.cloned.1.call-start = ((), (), s32[]{:S(2)}) async-start(), calls=%async_computation.2 | async-start | bytes 3317760 | tf_op jit(solution)/shard_map/reduce_scatter | solution.py:102
  62.0 2.7 copy-start.2
  62.0 207.0 %copy-start.7 = (f32[16]{0:T(128)S(1)}, f32[16]{0:T(128)}, u32[]{:S(2)}) copy-start(f32[16]{0:T(128)} %param.19) | copy-start | bytes 196
  62.0 207.2 %copy-start.6 = (s32[8]{0:T(128)S(1)}, s32[8]{0:T(128)}, u32[]{:S(2)}) copy-start(s32[8]{0:T(128)} %param.18) | copy-start | bytes 100
  269.0 25.6 %copy-start.5 = (f32[16]{0:T(128)}, f32[16]{0:T(128)S(1)}, u32[]{:S(2)}) copy-start(f32[16]{0:T(128)S(1)} %divide_subtract_fusion) | copy-start | bytes 196
  294.6 117.3 %copy-start.3 = (bf16[256,2880]{1,0:T(8,128)(2,1)S(1)}, bf16[256,2880]{1,0:T(8,128)(2,1)}, u32[]{:S(2)}) copy-start(bf16[256,2880]{1,0:T(8,128)(2,1)} %all-gather.9.cloned.1.call-done) | copy-start | bytes 4423684
  294.6 122.3 %reduce-scatter.7.cloned.1.call-start = ((), (), s32[]{:S(2)}) async-start(), calls=%async_computation.4 | async-start | bytes 491520 | tf_op jit(solution)/shard_map/reduce_scatter | solution.py:103
Sparse Core Ops, SparseCore 0:
  13.7 20.3 all-gather.8
  294.7 73.1 reduce-scatter.4
  370.6 21.0 reduce-scatter.6
where the time goes:
time: 430 us; the launch traced here: 426 us
  blocking collectives  237 us (55%)
  waiting for transfers between devices  84.7 us (20%)
  matrix products  54.8 us (13%)
  local copies, waits for them, and re-layouts  21.9 us (5%)
  between operations  14 us (3%)
  other arithmetic  12.5 us (3%)
    all_gather x3, blocking collectives, merged(): pieces = jax.tree.map(lambda part: lax.all_gather(part, axis), value)  192 us
    reduce_scatter x1, waiting for transfers between devices, on_device(): lax.psum_scatter(partial_grad, 'voc', scatter_dimension=1, tiled=True)  73.2 us
    psum x1, blocking collectives, on_device(): lax.psum(adapter_scale * contract_dims(logit_gradient, adapter_up, 1, 1),...  39.5 us
    dot_general x5, matrix products, contract_dims(): lax.dot_general(left, right, (((left_dim,), (right_dim,)), ((), ())), pre...  26.9 us
    dot_general x1, matrix products, on_device(): jnp.dot(gathered_rows, frozen_head_weight, preferred_element_type=jnp.flo...  21.9 us
    all_gather x1, waiting for transfers between devices, on_device(): gathered_rows = lax.all_gather(local_rows, 'tok', axis=0, tiled=True)  11.5 us
  transfers between devices with their start and end apart: 3, of which 2 were waited for; matrix products, arithmetic and copies ran while one was open for 3% of the time, Pallas kernels for 0%

commit v1 on v0

v1 whole, which is shorter than its diff:
```python
import functools

import jax
import jax.numpy as jnp
from jax import lax
from jax.experimental import pallas as pl
from jax.experimental.pallas import tpu as pltpu
from jax.sharding import PartitionSpec as P

MESH = pl.DeviceIdType.MESH
f32 = jnp.float32
bf16 = jnp.bfloat16
adapter_scale = 2.0
target_margin = 10.0
CORES = 2
Z_CHIPS = 4
KSTEP = 512
NSTEP = 256
VSTEP = 1024
LANES = 128


def dot_nn(a, b):
    return lax.dot_general(a, b, (((1,), (0,)), ((), ())), preferred_element_type=f32)


def dot_nt(a, b):
    return lax.dot_general(a, b, (((1,), (1,)), ((), ())), preferred_element_type=f32)


def dot_tn(a, b):
    return lax.dot_general(a, b, (((0,), (0,)), ((), ())), preferred_element_type=f32)


def eye_mask(n):
    return lax.broadcasted_iota(jnp.int32, (n, n), 0) == lax.broadcasted_iota(jnp.int32, (n, n), 1)


def to_col(row):
    n = row.shape[1]
    return jnp.sum(jnp.where(eye_mask(n), jnp.broadcast_to(row, (n, n)), 0.0), axis=1, keepdims=True)


def to_row(col):
    n = col.shape[0]
    return jnp.sum(jnp.where(eye_mask(n), jnp.broadcast_to(col, (n, n)), 0.0), axis=0, keepdims=True)


def kernel(
    cfg,
    ht,
    w,
    adt,
    adloc,
    au,
    tgt,
    seg,
    rsp,
    cf,
    refl,
    lr_out,
    hg_out,
    adg_out,
    aug_out,
    wv,
    lg,
    probs,
    xa,
    xl,
    lab,
    st,
    mx,
    sm,
    tm,
    g,
    sb,
    ra,
    tb,
    rb,
    ub,
    rc,
    yb,
    yr,
    lp,
    w_sem,
    xs_sem,
    xr_sem,
    ls_sem,
    lr_sem,
    ss_sem,
    sr_sem,
    as_sem,
    ar_sem,
    bs_sem,
    br_sem,
    cs_sem,
    cr_sem,
    ys_sem,
    yr_sem,
    ps_sem,
    pr_sem,
):
    NT, NV, X, Y, Z, S, V, D, K = cfg
    ND = NT * NV
    R = NT * S
    half = Y * S
    FW = D // NV
    LR = K // X
    tok = lax.axis_index("tok")
    voc = lax.axis_index("voc")
    y, core = tok // CORES, tok % CORES
    z, x = voc // X, voc % X
    me = tok * NV + voc
    sib = y * CORES + (1 - core)
    kst = list(range(0, D, KSTEP))
    nk = len(kst)
    dpad = xa.shape[1]

    def w_copy(i):
        size = min(KSTEP, D - kst[i])
        return pltpu.make_async_copy(
            w.at[pl.ds(kst[i], size), :], wv.at[pl.ds(kst[i], size), :], w_sem.at[i]
        )

    au_copy = pltpu.make_async_copy(au, wv.at[pl.ds(D, K), :], w_sem.at[nk])
    for i in range(nk):
        w_copy(i).start()
    au_copy.start()

    barrier = pltpu.get_barrier_semaphore()

    @pl.loop(1, ND)
    def _(d):
        peer = lax.rem(me + d, ND)
        pl.semaphore_signal(barrier, inc=1, device_id=(peer // NV, peer % NV), device_id_type=MESH)

    rows = ht.shape[1]
    resp = rsp[...]
    tri = (
        lax.broadcasted_iota(jnp.int32, (rows, rows), 0)
        <= lax.broadcasted_iota(jnp.int32, (rows, rows), 1)
    ).astype(bf16)
    before = dot_nn(jnp.broadcast_to(resp.astype(f32), (8, rows)).astype(bf16), tri)[0:1, :]
    position = before.astype(jnp.int32) - 1
    pick = (position == lax.broadcasted_iota(jnp.int32, (S, rows), 0)) & (resp > 0)
    pick_b = pick.astype(f32).astype(bf16)
    myrow = pl.multiple_of(core * half + y * S, S)
    xa[pl.ds(myrow, S), 0:D] = dot_nt(pick_b, ht[...]).astype(bf16)
    if dpad > D:
        xa[pl.ds(myrow, S), D:dpad] = jnp.zeros((S, dpad - D), bf16)
    lane = lax.broadcasted_iota(jnp.int32, (S, LANES), 1)
    t_col = jnp.sum(jnp.where(pick, tgt[...], 0), axis=1, keepdims=True)
    s_col = jnp.sum(jnp.where(pick, seg[...], 0), axis=1, keepdims=True)
    l_col = jnp.sum(jnp.where(pick, 1, 0), axis=1, keepdims=True)
    lab[pl.ds(myrow, S), :] = jnp.where(
        lane == 0, t_col, jnp.where(lane == 1, s_col, jnp.where(lane == 2, l_col, 0))
    )

    pl.semaphore_wait(barrier, ND - 1)

    def x_ref(i, yy, cc):
        size = min(KSTEP, dpad - kst[i])
        r0 = pl.multiple_of(cc * half + yy * S, S)
        return xa.at[pl.ds(r0, S), pl.ds(kst[i], size)]

    def x_copy(i, slot, yy, cc, dev):
        ref = x_ref(i, yy, cc)
        return pltpu.make_async_remote_copy(
            ref, ref, xs_sem.at[i, slot], xr_sem.at[i, slot], device_id=(dev, voc), device_id_type=MESH
        )

    def x_direct(i, dy):
        return x_copy(i, dy, y, core, lax.rem(y + dy, Y) * CORES + core)

    def x_recv(i, slot, yy, cc):
        return x_copy(i, slot, yy, cc, sib)

    def lab_copy(slot, yy, cc, dev):
        r0 = pl.multiple_of(cc * half + yy * S, S)
        ref = lab.at[pl.ds(r0, S), :]
        return pltpu.make_async_remote_copy(
            ref, ref, ls_sem.at[slot], lr_sem.at[slot], device_id=(dev, voc), device_id_type=MESH
        )

    for i in range(nk):
        for dy in range(1, Y):
            x_direct(i, dy).start()
        x_copy(i, 0, y, core, sib).start()
    for d in range(1, NT):
        lab_copy(d, y, core, lax.rem(tok + d, NT)).start()

    def y_from(dy):
        return lax.rem(y + Y - dy, Y)

    def forward(i):
        for dy in range(1, Y):
            x_recv(i, dy, y_from(dy), core).wait_recv()
            x_copy(i, Y - 1 + dy, y_from(dy), core, sib).start()

    def arrive(i):
        x_recv(i, 0, y, 1 - core).wait_recv()
        for dy in range(1, Y):
            x_recv(i, Y - 1 + dy, y_from(dy), 1 - core).wait_recv()

    nfull = V // NSTEP
    vtail = V - nfull * NSTEP
    mx[...] = jnp.full(mx.shape, -jnp.inf, f32)
    sm[...] = jnp.zeros(sm.shape, f32)
    tm[...] = jnp.zeros(tm.shape, f32)

    def folded(tile, op):
        out = tile[:, 0:LANES]
        for j in range(1, NSTEP // LANES):
            out = op(out, tile[:, j * LANES : (j + 1) * LANES])
        return out

    forward(0)
    tail_max = None
    for i in range(nk):
        last = i == nk - 1
        if not last:
            forward(i + 1)
        arrive(i)
        w_copy(i).wait()
        if last:
            size = D - kst[i]
            au_copy.wait()
            acc = dot_nt(xa[:, 0:D], adt[...])
            xl[:, 0:size] = xa[:, kst[i] : D]
            xl[:, size : size + K] = (adapter_scale * acc.astype(bf16).astype(f32)).astype(bf16)
            lhs = xl
            lcols = slice(0, size + K)
            wrows = slice(kst[i], D + K)
        else:
            lhs = xa
            lcols = slice(kst[i], kst[i] + KSTEP)
            wrows = slice(kst[i], kst[i] + KSTEP)

        def step(n, carry, i=i, last=last, lhs=lhs, lcols=lcols, wrows=wrows):
            cols = pl.ds(pl.multiple_of(n * NSTEP, NSTEP), NSTEP)
            tile = dot_nn(lhs[:, lcols], wv[wrows, cols])
            if i > 0:
                tile = tile + lg[:, cols]
            lg[:, cols] = tile
            if last:
                mx[...] = jnp.maximum(mx[...], folded(tile, jnp.maximum))
            return carry

        lax.fori_loop(0, nfull, step, 0)
        if vtail:
            cols = slice(nfull * NSTEP, V)
            tile = dot_nn(lhs[:, lcols], wv[wrows, cols])
            if i > 0:
                tile = tile + lg[:, cols]
            lg[:, cols] = tile
            if last:
                tail_max = jnp.max(tile, axis=1, keepdims=True)

    peak = jnp.max(mx[...], axis=1, keepdims=True)
    if vtail:
        peak = jnp.maximum(peak, tail_max)

    for d in range(1, NT):
        src = lax.rem(tok + NT - d, NT)
        lab_copy(d, src // CORES, src % CORES, sib).wait_recv()
    labels = lab[...]
    target = labels[:, 0:1]
    segs = labels[:, 1:2]
    live = labels[:, 2:3].astype(f32)
    slot_col = jnp.where(live > 0, target - me * V, -1)

    def exp_tile(cols, first, width):
        tile = lg[:, cols]
        hit = (lax.broadcasted_iota(jnp.int32, (R, width), 1) + first) == slot_col
        e = jnp.exp(tile - peak)
        lg[:, cols] = e
        return e, jnp.where(hit, tile, 0.0)

    def exp_step(n, carry):
        cols = pl.ds(pl.multiple_of(n * NSTEP, NSTEP), NSTEP)
        e, t = exp_tile(cols, n * NSTEP, NSTEP)
        sm[...] += folded(e, jnp.add)
        tm[...] += folded(t, jnp.add)
        return carry

    lax.fori_loop(0, nfull, exp_step, 0)
    summed = jnp.sum(sm[...], axis=1, keepdims=True)
    picked = jnp.sum(tm[...], axis=1, keepdims=True)
    if vtail:
        e, t = exp_tile(slice(nfull * NSTEP, V), nfull * NSTEP, vtail)
        summed = summed + jnp.sum(e, axis=1, keepdims=True)
        picked = picked + jnp.sum(t, axis=1, keepdims=True)

    nr = R // LANES
    st[pl.ds(me, 1)] = jnp.zeros((1,) + st.shape[1:], f32)
    for j, col in enumerate((peak, summed, picked)):
        for r in range(nr):
            st[me, j * nr + r : j * nr + r + 1, :] = to_row(col[r * LANES : (r + 1) * LANES, :])

    def st_copy(d, slot):
        peer = lax.rem(me + d, ND)
        return pltpu.make_async_remote_copy(
            st.at[slot],
            st.at[slot],
            ss_sem.at[d],
            sr_sem.at[d],
            device_id=(peer // NV, peer % NV),
            device_id_type=MESH,
        )

    @pl.loop(1, ND)
    def _(d):
        st_copy(d, me).start()

    @pl.loop(1, ND)
    def _(d):
        st_copy(d, lax.rem(me + ND - d, ND)).wait_recv()

    stats = st[...]
    m_all = stats[:, 0:nr, :]
    top = jnp.max(m_all, axis=0)
    total = jnp.sum(stats[:, nr : 2 * nr, :] * jnp.exp(m_all - top[None]), axis=0)
    hit_logit = jnp.sum(stats[:, 2 * nr : 3 * nr, :], axis=0)
    norm = top + jnp.log(total)
    logp = hit_logit - norm
    norm_col = jnp.concatenate([to_col(norm[r : r + 1, :]) for r in range(nr)], axis=0)
    logp_col = jnp.concatenate([to_col(logp[r : r + 1, :]) for r in range(nr)], axis=0)

    nseq = refl.shape[1]
    seq_lane = lax.broadcasted_iota(jnp.int32, (R, LANES), 1)
    mine = (segs == seq_lane) & (live > 0)
    counts = jnp.sum(jnp.where(mine, 1.0, 0.0), axis=0, keepdims=True)
    totals = jnp.sum(jnp.where(mine, logp_col, 0.0), axis=0, keepdims=True)
    counts = jnp.where(counts > 0, counts, 1.0)
    ratio = (totals / counts)[:, 0:nseq] - refl[...]
    lr_out[...] = ratio
    ratio_c = jnp.broadcast_to(ratio, (nseq, nseq))
    si = lax.broadcasted_iota(jnp.int32, (nseq, nseq), 0)
    sj = lax.broadcasted_iota(jnp.int32, (nseq, nseq), 1)
    ratio_col = jnp.sum(jnp.where(si == sj, ratio_c, 0.0), axis=1, keepdims=True)
    other = (si // 2 == sj // 2) & (si != sj)
    ratio_other = jnp.sum(jnp.where(other, jnp.broadcast_to(ratio_col, (nseq, nseq)), 0.0), axis=0, keepdims=True)
    npair = nseq // 2
    pi = lax.broadcasted_iota(jnp.int32, (npair, npair), 0)
    pj = lax.broadcasted_iota(jnp.int32, (npair, npair), 1)
    first_c = jnp.sum(
        jnp.where(pi == pj, jnp.broadcast_to(cf[...], (npair, npair)), 0), axis=1, keepdims=True
    )
    qi = lax.broadcasted_iota(jnp.int32, (npair, nseq), 0)
    qj = lax.broadcasted_iota(jnp.int32, (npair, nseq), 1)
    first = jnp.sum(jnp.where(qi == qj // 2, first_c, 0), axis=0, keepdims=True)
    even = (lax.broadcasted_iota(jnp.int32, (1, nseq), 1) % 2) == 0
    sign = jnp.where((first == 1) == even, 1.0, -1.0)
    margin = sign * (ratio - ratio_other)
    seq_weight = sign * 2.0 * (margin - target_margin) / counts[:, 0:nseq]
    member = (segs == lax.broadcasted_iota(jnp.int32, (R, nseq), 1)) & (live > 0)
    weight = jnp.sum(jnp.where(member, seq_weight, 0.0), axis=1, keepdims=True)
    scale = jnp.exp(peak - norm_col)

    size = D - kst[-1]
    lora = xl[:, size : size + K]
    eye_k = eye_mask(K).astype(f32).astype(bf16)
    lora_t = dot_nt(eye_k, lora).astype(bf16)

    def grad_tile(cols, first_col, width):
        hit = (lax.broadcasted_iota(jnp.int32, (R, width), 1) + first_col) == slot_col
        p = lg[:, cols] * scale
        gr = (weight * jnp.where(hit, p - 1.0, p)).astype(bf16)
        probs[:, cols] = gr
        aug_out[:, cols] = dot_nn(lora_t, gr)

    def grad_step(n, carry):
        grad_tile(pl.ds(pl.multiple_of(n * NSTEP, NSTEP), NSTEP), n * NSTEP, NSTEP)
        return carry

    lax.fori_loop(0, nfull, grad_step, 0)
    if vtail:
        grad_tile(slice(nfull * NSTEP, V), nfull * NSTEP, vtail)

    order = [Z - 1] + list(range(Z - 1))
    vfull = V // VSTEP
    ktail = V - vfull * VSTEP
    CH = X * FW
    F = sb.shape[2]
    keep = pl.multiple_of(core * half, LANES)
    give = pl.multiple_of((1 - core) * half, LANES)

    def product(i):
        q = order[i]
        extra = K if q == Z - 1 else 0
        r0, size = q * CH, CH + extra
        if ktail:
            g[0:size, :] = dot_nt(wv[r0 : r0 + size, vfull * VSTEP : V], probs[:, vfull * VSTEP : V])
        else:
            g[0:size, :] = jnp.zeros((size, R), f32)

        def body(n, carry):
            cols = pl.ds(pl.multiple_of(n * VSTEP, VSTEP), VSTEP)
            g[0:size, :] += dot_nt(wv[r0 : r0 + size, cols], probs[:, cols])
            return carry

        lax.fori_loop(0, vfull, body, 0)
        for xx in range(X):
            sb[i, xx, 0:FW, :] = g[xx * FW : (xx + 1) * FW, :].astype(bf16)
            if extra:
                sb[i, xx, FW : FW + LR, :] = (
                    adapter_scale * g[CH + xx * LR : CH + (xx + 1) * LR, :]
                ).astype(bf16)
                if F > FW + LR:
                    sb[i, xx, FW + LR : F, :] = jnp.zeros((F - FW - LR, R), bf16)
            elif F > FW:
                sb[i, xx, FW:F, :] = jnp.zeros((F - FW, R), bf16)

    def a_copy(i):
        return pltpu.make_async_remote_copy(
            sb.at[i, :, :, pl.ds(give, half)],
            ra.at[i],
            as_sem.at[i],
            ar_sem.at[i],
            device_id=(sib, voc),
            device_id_type=MESH,
        )

    def b_copy(i, dx):
        px = lax.rem(x + dx, X)
        return pltpu.make_async_remote_copy(
            tb.at[i, px],
            rb.at[i, dx - 1],
            bs_sem.at[i, dx],
            br_sem.at[i, dx],
            device_id=(tok, z * X + px),
            device_id_type=MESH,
        )

    def stage_b(i):
        a_copy(i).wait_recv()
        tb[i] = (sb[i, :, :, pl.ds(keep, half)].astype(f32) + ra[i].astype(f32)).astype(bf16)
        for dx in range(1, X):
            b_copy(i, dx).start()

    def c_copy(i, slot):
        return pltpu.make_async_remote_copy(
            ub.at[i],
            rc.at[slot],
            cs_sem.at[i],
            cr_sem.at[slot],
            device_id=(tok, order[i] * X + x),
            device_id_type=MESH,
        )

    def stage_c(i):
        q = order[i]
        total_c = tb[i, x].astype(f32)
        for dx in range(1, X):
            b_copy(i, dx).wait_recv()
            total_c = total_c + rb[i, dx - 1].astype(f32)
        ub[i] = total_c.astype(bf16)

        @pl.when(z != q)
        def _():
            c_copy(i, lax.rem(z + Z - q, Z) - 1).start()

    def y_copy(dy):
        py = lax.rem(y + dy, Y)
        return pltpu.make_async_remote_copy(
            yb.at[py],
            yr.at[dy - 1],
            ys_sem.at[dy],
            yr_sem.at[dy],
            device_id=(py * CORES + core, voc),
            device_id_type=MESH,
        )

    def stage_d(i):
        @pl.when(z == order[i])
        def _():
            total_d = ub[i].astype(f32)
            for j in range(Z - 1):
                pltpu.make_async_remote_copy(
                    ub.at[i],
                    rc.at[j],
                    cs_sem.at[i],
                    cr_sem.at[j],
                    device_id=(sib, voc),
                    device_id_type=MESH,
                ).wait_recv()
                total_d = total_d + rc[j].astype(f32)
            total_d = total_d.astype(bf16)
            for yy in range(Y):
                yb[yy, :, 0:S] = total_d[:, yy * S : (yy + 1) * S]
                yb[yy, :, S:LANES] = jnp.zeros((F, LANES - S), bf16)
            for dy in range(1, Y):
                y_copy(dy).start()

    def y_total():
        out = yb[y].astype(f32)
        for dy in range(1, Y):
            out = out + yr[dy - 1].astype(f32)
        return out

    def lp_copy(d, s_tok, s_x):
        peer = lax.rem(me + d, ND)
        ref = lp.at[s_tok, s_x]
        return pltpu.make_async_remote_copy(
            ref,
            ref,
            ps_sem.at[d],
            pr_sem.at[s_tok, s_x],
            device_id=(peer // NV, peer % NV),
            device_id_type=MESH,
        )

    def lora_send():
        @pl.when(z == Z - 1)
        def _():
            for dy in range(1, Y):
                y_copy(dy).wait_recv()
            piece = y_total()[FW : FW + LR, :]
            lp[tok, x, 0:LR, :] = piece.astype(bf16)
            if lp.shape[2] > LR:
                lp[tok, x, LR:, :] = jnp.zeros((lp.shape[2] - LR, LANES), bf16)

            @pl.loop(1, ND)
            def _(d):
                lp_copy(d, tok, x).start()

    for i in range(Z):
        product(i)
        a_copy(i).start()
        if i >= 1:
            stage_b(i - 1)
        if i >= 2:
            stage_c(i - 2)
        if i >= 3:
            stage_d(i - 3)
    stage_b(Z - 1)
    if Z >= 2:
        stage_c(Z - 2)
    if Z < 4:
        for i in range(max(0, Z - 3), Z - 1):
            stage_d(i)
    else:
        stage_d(Z - 3)
    lora_send()
    stage_c(Z - 1)
    if Z >= 4:
        stage_d(Z - 2)
    stage_d(Z - 1)

    @pl.when(z != Z - 1)
    def _():
        for dy in range(1, Y):
            y_copy(dy).wait_recv()

    for s_tok in range(NT):
        for s_x in range(X):

            @pl.when(me != s_tok * NV + (Z - 1) * X + s_x)
            def _(s_tok=s_tok, s_x=s_x):
                lp_copy(1, s_tok, s_x).wait_recv()

    pieces = []
    for cc in range(CORES):
        for yy in range(Y):
            pieces.append(
                jnp.concatenate(
                    [lp[yy * CORES + cc, s_x].astype(f32)[0:LR, 0:S] for s_x in range(X)], axis=0
                )
            )
    lora_grad_t = jnp.concatenate(pieces, axis=1).astype(bf16)
    adg_out[...] = dot_nn(lora_grad_t, xa[:, 0:D])
    my_lora_t = jnp.concatenate(
        [lp[tok, s_x].astype(f32)[0:LR, 0:S] for s_x in range(X)], axis=0
    ).astype(bf16)
    slots = y_total()[0:FW, 0:S] + dot_nn(adloc[...], my_lora_t)
    hg_out[...] = dot_nn(slots.astype(bf16), pick_b).astype(bf16)

    for i in range(nk):
        for dy in range(1, Y):
            x_direct(i, dy).wait_send()
            x_copy(i, Y - 1 + dy, y_from(dy), core, sib).wait_send()
        x_copy(i, 0, y, core, sib).wait_send()
    for d in range(1, NT):
        lab_copy(d, y, core, lax.rem(tok + d, NT)).wait_send()

    @pl.loop(1, ND)
    def _(d):
        st_copy(d, me).wait_send()

    for i in range(Z):
        a_copy(i).wait_send()
        for dx in range(1, X):
            b_copy(i, dx).wait_send()

        @pl.when(z != order[i])
        def _(i=i):
            c_copy(i, lax.rem(z + Z - order[i], Z) - 1).wait_send()

    for dy in range(1, Y):
        y_copy(dy).wait_send()

    @pl.when(z == Z - 1)
    def _():
        @pl.loop(1, ND)
        def _(d):
            lp_copy(d, tok, x).wait_send()


def up(n, m):
    return -(-n // m) * m


def on_device(hidden, weight, adapter_down, adapter_up, targets, segment, response, chosen_first, reference_logp):
    NT = lax.axis_size("tok")
    NV = lax.axis_size("voc")
    ND = NT * NV
    Z = Z_CHIPS
    X, Y = NV // Z, NT // CORES
    rows, D = hidden.shape
    S = rows // 2
    V = weight.shape[1]
    K = adapter_down.shape[1]
    R = NT * S
    FW = D // NV
    LR = K // X
    F = up(FW + LR, 16)
    half = Y * S
    dpad = up(D, LANES)
    nk = len(range(0, D, KSTEP))
    cfg = (NT, NV, X, Y, Z, S, V, D, K)
    adloc = lax.dynamic_slice_in_dim(adapter_down, lax.axis_index("voc") * FW, FW, 0)
    vm = pl.BlockSpec(memory_space=pltpu.VMEM)
    hbm = pl.BlockSpec(memory_space=pl.ANY)
    dma = pltpu.SemaphoreType.DMA
    ratio, hg_t, adg_t, aug = pl.pallas_call(
        functools.partial(kernel, cfg),
        out_shape=(
            jax.ShapeDtypeStruct((1, reference_logp.shape[0]), f32),
            jax.ShapeDtypeStruct((FW, rows), bf16),
            jax.ShapeDtypeStruct((K, D), f32),
            jax.ShapeDtypeStruct((K, V), f32),
        ),
        in_specs=[vm, hbm, vm, vm, hbm, vm, vm, vm, vm, vm],
        out_specs=(vm, vm, vm, vm),
        scratch_shapes=[
            pltpu.VMEM((D + K, V), bf16),
            pltpu.VMEM((R, V), f32),
            pltpu.VMEM((R, V), bf16),
            pltpu.VMEM((R, dpad), bf16),
            pltpu.VMEM((R, up(KSTEP + K, LANES)), bf16),
            pltpu.VMEM((R, LANES), jnp.int32),
            pltpu.VMEM((ND, up(3 * R // LANES, 8), LANES), f32),
            pltpu.VMEM((R, LANES), f32),
            pltpu.VMEM((R, LANES), f32),
            pltpu.VMEM((R, LANES), f32),
            pltpu.VMEM((X * FW + K, R), f32),
            pltpu.VMEM((Z, X, F, R), bf16),
            pltpu.VMEM((Z, X, F, half), bf16),
            pltpu.VMEM((Z, X, F, half), bf16),
            pltpu.VMEM((Z, max(X - 1, 1), F, half), bf16),
            pltpu.VMEM((Z, F, half), bf16),
            pltpu.VMEM((Z - 1, F, half), bf16),
            pltpu.VMEM((Y, F, LANES), bf16),
            pltpu.VMEM((max(Y - 1, 1), F, LANES), bf16),
            pltpu.VMEM((NT, X, up(LR, 16), LANES), bf16),
            dma((nk + 1,)),
            dma((nk, 2 * Y)),
            dma((nk, 2 * Y)),
            dma((NT,)),
            dma((NT,)),
            dma((ND,)),
            dma((ND,)),
            dma((Z,)),
            dma((Z,)),
            dma((Z, X)),
            dma((Z, X)),
            dma((Z,)),
            dma((Z,)),
            dma((Y,)),
            dma((Y,)),
            dma((ND,)),
            dma((NT, X)),
        ],
        compiler_params=pltpu.CompilerParams(
            collective_id=0, has_side_effects=True, vmem_limit_bytes=62 * 1024 * 1024
        ),
    )(
        hidden.T,
        weight,
        adapter_down.T,
        adloc,
        adapter_up,
        targets.reshape(1, -1),
        segment.reshape(1, -1),
        response.reshape(1, -1),
        chosen_first.reshape(1, -1),
        reference_logp.reshape(1, -1),
    )
    return ratio.reshape(-1), hg_t.T, adg_t.T, aug


def solution(mesh):
    in_specs = (
        P("tok", None),
        P(None, ("tok", "voc")),
        P(),
        P(None, ("tok", "voc")),
        P("tok"),
        P("tok"),
        P("tok"),
        P(),
        P(),
    )
    out_specs = (P(), P("tok", "voc"), P(), P(None, ("tok", "voc")))
    return jax.shard_map(
        on_device, mesh=mesh, in_specs=in_specs, out_specs=out_specs, check_vma=False
    )
```

time: 430 us -> 106 us (0.25)
  blocking collectives: 237 us -> 0 us
  Pallas kernels: 0 us -> 97.3 us
  waiting for transfers between devices: 84.7 us -> 0 us
  matrix products: 54.8 us -> 0 us
  local copies, waits for them, and re-layouts: 21.9 us -> 8.12 us
  between operations: 14 us -> 0.64 us
  other arithmetic: 12.5 us -> 0 us
    all_gather x4 -> x0, blocking collectives: 198 us -> none  [the longest x3 192 us: merged(): pieces = jax.tree.map(lambda part: lax.all_gather(part, axis), value)]
    pallas_call x0 -> x1, Pallas kernels: none -> 97.3 us  [on_device(): pl.pallas_call(functools.partial(kernel, cfg), out_shape=(jax.ShapeDtypeS...]
    reduce_scatter x2 -> x0, waiting for transfers between devices: 73.2 us -> none  [the longest x1 73.2 us: on_device(): lax.psum_scatter(partial_grad, 'voc', scatter_dimension=1, tiled=True)]
    dot_general x8 -> x0, matrix products: 54.8 us -> none  [the longest x5 26.9 us: contract_dims(): lax.dot_general(left, right, (((left_dim,), (right_dim,)), ((), ())), pre...]
    psum x1 -> x0, blocking collectives: 39.5 us -> none  [on_device(): lax.psum(adapter_scale * contract_dims(logit_gradient, adapter_up, 1, 1),...]
    gather x5 -> x0, local copies, waits for them, and re-layouts: 13.1 us -> none  [the longest x1 7.98 us: on_device(): jnp.take_along_axis(logit_matrix, column_slot[:, None], axis=1)[:, 0]]
    all_gather x1 -> x0, waiting for transfers between devices: 11.5 us -> none  [on_device(): gathered_rows = lax.all_gather(local_rows, 'tok', axis=0, tiled=True)]
    convert_element_type x2 -> x0, other arithmetic: 6.78 us -> none  [the longest x1 6.76 us: on_device(): (row_weight[:, None] * (predicted - hits.astype(jnp.float32))).astype(jnp...]
  transfers between devices with their start and end apart: 3 -> 0, of which waited for: 2 -> 0; matrix products, arithmetic and copies ran while one was open for 3% -> 0% of each run, Pallas kernels for 0% -> 0%
where the time goes in v1:
time: 106 us
  Pallas kernels  97.3 us (92%)
  local copies, waits for them, and re-layouts  8.12 us (8%)
    pallas_call x1, Pallas kernels, on_device(): pl.pallas_call(functools.partial(kernel, cfg), out_shape=(jax.ShapeDtypeS...  97.3 us
    unnamed x5, local copies, waits for them, and re-layouts  7.27 us

profile of v1, /device:TPU:16, one launch (start us, length us, event | category | flops | bytes accessed | tf_op | source)
XLA Modules:
  0.0 106.0 jit_solution(4137990549881296314)
XLA Ops:
  0.6 0.8 constant_dynamic-slice_fusion
  1.5 0.8 copy.14.adloc
  2.2 97.3 %shard_map.120 = (f32[1,16]{1,0:T(1,128)}, bf16[360,128]{1,0:T(8,128)(2,1)}, f32[32,2880]{1,0:T(8,128)}, f32[32,6284]{1,0:T(8,128)}) custom-call(bf16[2880,128]{1,0:T(8,128)(2,1)} %bitcast.10, bf16[2880,6284]{1,0:T(8,128)(2,1)} %w.1, bf16[32,2880]{1,0:T(8,128)(2,1)} %bitcast.12, bf16[360,32]{1,0:T(8,128)(2,1)} %copy.14.adloc, bf16[32,6284]{1,0:T(8,128)(2,1)} %au.1, ...), custom_call_target="tpu_custom_call" | custom-call | tf_op jit(solution)/shard_map/pallas_call | solution.py:635
  99.5 1.1 %copy.19 = f32[16]{0:T(128)} copy(f32[16]{0:T(128)} %bitcast.19) | data formatting | bytes 128
  100.7 1.5 %copy.20 = bf16[128,360]{0,1:T(8,128)(2,1)} copy(bf16[128,360]{0,1:T(8,128)(2,1)} %bitcast.13) | data formatting | bytes 184320
  102.2 1.8 %copy.21 = f32[2880,32]{0,1:T(8,128)} copy(f32[2880,32]{0,1:T(8,128)} %bitcast.11) | data formatting | bytes 737280
  104.0 2.1 %copy.22 = f32[32,6284]{1,0:T(8,128)} copy(f32[32,6284]{1,0:T(8,128)} %get-tuple-element.19) | data formatting | bytes 1608704

commit v2 on v1

--- a/solution.py
+++ b/solution.py
@@ -14,10 +14,16 @@
 target_margin = 10.0
 CORES = 2
 Z_CHIPS = 4
-KSTEP = 512
-NSTEP = 256
-VSTEP = 1024
+KSTEP = 1024
+NSTEP_MAX = 2048
+VSTEP_MAX = 3072
 LANES = 128
+
+
+def fit(step, limit):
+    while step > limit:
+        step //= 2
+    return step
 
 
 def dot_nn(a, b):
@@ -101,6 +107,7 @@
     pr_sem,
 ):
     NT, NV, X, Y, Z, S, V, D, K = cfg
+    NSTEP, VSTEP = fit(NSTEP_MAX, V), fit(VSTEP_MAX, V)
     ND = NT * NV
     R = NT * S
     half = Y * S

time: 106 us -> 80.8 us (0.76)
  Pallas kernels: 97.3 us -> 71.7 us
    pallas_call x1, Pallas kernels: 97.3 us -> 71.7 us  [on_device(): pl.pallas_call(functools.partial(kernel, cfg), out_shape=(jax.ShapeDtypeS...]
where the time goes in v2:
time: 80.8 us; the launch traced here: 80.5 us
  Pallas kernels  71.7 us (89%)
  local copies, waits for them, and re-layouts  8.12 us (10%)
    pallas_call x1, Pallas kernels, on_device(): pl.pallas_call(functools.partial(kernel, cfg), out_shape=(jax.ShapeDtypeS...  71.7 us
    unnamed x5, local copies, waits for them, and re-layouts  7.27 us

profile of v2, /device:TPU:16, one launch (start us, length us, event | category | flops | bytes accessed | tf_op | source)
XLA Modules:
  0.0 80.5 jit_solution(15319567698160611182)
XLA Ops:
  0.6 0.8 %constant_dynamic-slice_fusion = bf16[360,32]{0,1:T(8,128)(2,1)S(1)} fusion(bf16[2880,32]{0,1:T(8,128)(2,1)} %param.11, s32[]{:T(128)S(6)} %select_n.3), kind=kLoop, calls=%fused_computation | loop fusion | bytes 46084 | tf_op jit(solution)/shard_map/dynamic_slice | solution.py:638
  1.5 0.8 copy.14.adloc
  2.2 71.7 %shard_map.120 = (f32[1,16]{1,0:T(1,128)}, bf16[360,128]{1,0:T(8,128)(2,1)}, f32[32,2880]{1,0:T(8,128)}, f32[32,6284]{1,0:T(8,128)}) custom-call(bf16[2880,128]{1,0:T(8,128)(2,1)} %bitcast.10, bf16[2880,6284]{1,0:T(8,128)(2,1)} %w.1, bf16[32,2880]{1,0:T(8,128)(2,1)} %bitcast.12, bf16[360,32]{1,0:T(8,128)(2,1)} %copy.14.adloc, bf16[32,6284]{1,0:T(8,128)(2,1)} %au.1, ...), custom_call_target="tpu_custom_call" | custom-call | tf_op jit(solution)/shard_map/pallas_call | solution.py:642
  74.0 1.1 %copy.19 = f32[16]{0:T(128)} copy(f32[16]{0:T(128)} %bitcast.19) | data formatting | bytes 128
  75.1 1.5 %copy.20 = bf16[128,360]{0,1:T(8,128)(2,1)} copy(bf16[128,360]{0,1:T(8,128)(2,1)} %bitcast.13) | data formatting | bytes 184320
  76.6 1.8 %copy.21 = f32[2880,32]{0,1:T(8,128)} copy(f32[2880,32]{0,1:T(8,128)} %bitcast.11) | data formatting | bytes 737280
  78.4 2.1 %copy.22 = f32[32,6284]{1,0:T(8,128)} copy(f32[32,6284]{1,0:T(8,128)} %get-tuple-element.19) | data formatting | bytes 1608704
